TPU v7x, 512 devices: a whole 4x8x8 slice. The times are simulated.
512 devices in a mesh: dp: 32 (over z, y_hi), tensor: 16 (over y_lo, x, core).
Axes of the slice: x: 4, y: 8 (y_hi: 4, y_lo: 2; y = y_hi * 2 + y_lo), z: 8, core: 2. Of those that a mesh axis runs over, the one named last changes fastest.
Arguments:
- activations: bfloat16 [256, 128, 8192], P('dp', None, 'tensor'), may hold values from -6 to 6
- cotangents: bfloat16 [256, 128, 8192], P('dp', None, 'tensor'), may hold values from -6 to 6
- lengths: int32 [256], P('dp'), may hold values from 32 to 128
- adapter_down_matrix: bfloat16 [8192, 8], P('tensor'), may hold values from -0.0625 to 0.0625
- adapter_up_matrix: bfloat16 [8, 8192], P(None, 'tensor'), may hold values from -0.0625 to 0.0625
- projection: bfloat16 [131072, 4096], P('tensor', 'dp'), may hold values from -0.015625 to 0.015625
- validation_gradient_rows: bfloat16 [256, 4096], P(None, 'dp'), may hold values from -6 to 6
Outputs:
- scores: float32 [256, 256], P('tensor')
All inputs are finite; a program needn't handle non-finite values.
Results may differ from a plain program's by a relative error of at most 0.0041.
Values may be sent and summed in bfloat16 or wider, within the bound.
A program may use at most 64 MiB of HBM per device.

v0:
```python
import math

import jax
import jax.numpy as jnp
from jax import lax
from jax.sharding import PartitionSpec as P

K = 4096


adapter_scale = 2.0
epsilon = 1e-06


def body(
    activations,
    cotangents,
    lengths,
    adapter_down_matrix,
    adapter_up_matrix,
    projection,
    validation_gradient_rows,
):
    examples = activations.shape[0]
    length_max = activations.shape[1]
    tensor_count = lax.axis_size("tensor")
    data_count = lax.axis_size("dp")
    target = validation_gradient_rows.astype(jnp.float32)
    target_sq = jnp.sum(target * target, axis=1)
    token_positions = lax.broadcasted_iota(jnp.int32, (examples, 1, length_max), 2)
    weight_values = (token_positions < lengths[:, None, None]).astype(jnp.float32) * adapter_scale
    down_part = jnp.einsum(
        "ijv,vw->iwj", activations, adapter_down_matrix, preferred_element_type=jnp.float32
    )
    up_portion = jnp.einsum(
        "fga,wa->fwg", cotangents, adapter_up_matrix, preferred_element_type=jnp.float32
    )
    down_hidden_state, up_hidden_state = lax.psum((down_part, up_portion), "tensor")
    left_factor = (weight_values * up_hidden_state).astype(jnp.bfloat16)
    right_factor = (weight_values * down_hidden_state).astype(jnp.bfloat16)
    grad_down = jnp.einsum(
        "esd,ers->edr", activations, left_factor, preferred_element_type=jnp.float32
    )
    grad_up = jnp.einsum(
        "esd,ers->edr", cotangents, right_factor, preferred_element_type=jnp.float32
    )
    gradients = (
        jnp.concatenate([grad_down, grad_up], axis=2).reshape(examples, -1).astype(jnp.bfloat16)
    )
    block_rows = examples * data_count // tensor_count
    partial_sum = jnp.dot(
        lax.all_gather(gradients, "dp", axis=0, tiled=True),
        projection,
        preferred_element_type=jnp.float32,
    )
    summed = lax.psum(partial_sum, "tensor")
    projected = lax.dynamic_slice_in_dim(
        summed, lax.axis_index("tensor") * block_rows, block_rows, 0
    )
    train_sq = jnp.sum(projected * projected, axis=1)
    inner = jnp.dot(
        projected, target.T, precision=lax.Precision.HIGHEST, preferred_element_type=jnp.float32
    )
    inner, train_sq, target_sq = lax.psum((inner, train_sq, target_sq), "dp")
    factor = math.sqrt(K)
    return (
        factor
        * inner
        * lax.rsqrt(train_sq + epsilon)[:, None]
        * lax.rsqrt(target_sq + epsilon)[None, :]
    )


def solution(mesh):
    placed = (
        P("dp", None, "tensor"),
        P("dp", None, "tensor"),
        P("dp"),
        P("tensor", None),
        P(None, "tensor"),
        P("tensor", "dp"),
        P(None, "dp"),
    )
    return jax.shard_map(
        body, mesh=mesh, in_specs=placed, out_specs=P("tensor", None), check_vma=False
    )
```

profile of v0, /device:TPU:6, one launch (start us, length us, event | category | flops | bytes accessed | tf_op | source)
XLA Modules:
  0.0 533.4 jit_solution(488176951012435388)
XLA Ops:
  6.5 0.0 copy-start
  6.5 0.0 all-reduce.7.cloned.1.call-start
  6.5 2.4 convolution_bitcast_fusion
  8.9 2.2 convolution_bitcast_fusion.1
  11.1 0.0 all-reduce.7.cloned.1.call-update
  11.2 0.0 all-gather.2.cloned.1.call-start
  11.2 0.7 fusion.8
  11.9 118.5 %all-reduce.7.cloned.1.call-done = (f32[8,8,128]{2,1,0:T(8,128)}, f32[8,8,128]{2,1,0:T(8,128)}) async-done(((f32[8,8,128]{2,1,0:T(8,128)}, f32[8,8,128]{2,1,0:T(8,128)}), (f32[8,8,128]{2,1,0:T(8,128)}, f32[8,8,128]{2,1,0:T(8,128)})) %all-reduce.7.cloned.1.call-update) | async-done | bytes 65552 | tf_op jit(solution)/shard_map/psum | solution.py:38
  130.5 1.5 fusion.1
  132.0 1.5 fusion
  133.5 0.5 copy.8
  134.0 0.0 copy-start.1
  134.0 2.4 convert_element_type.16
  136.4 0.0 all-gather.2.cloned.1.call-update
  136.4 0.0 all-reduce.5.cloned.1.call-start
  136.5 106.5 %all-gather.2.cloned.1.call-done = bf16[256,8192]{1,0:T(8,128)(2,1)} async-done(((bf16[8,8192]{1,0:T(8,128)(2,1)}), bf16[256,8192]{1,0:T(8,128)(2,1)}) %all-gather.2.cloned.1.call-update) | async-done | bytes 4194320 | tf_op jit(solution)/shard_map/all_gather | solution.py:52
  243.0 0.0 copy-done
  243.0 4.1 fusion.10
  247.1 0.0 all-reduce.5.cloned.1.call-update
  247.1 0.0 copy-done.1
  247.1 0.1 multiply_reduce_fusion
  247.3 118.8 %all-reduce.5.cloned.1.call-done = f32[256,128]{1,0:T(8,128)} async-done(((f32[256,128]{1,0:T(8,128)}), f32[256,128]{1,0:T(8,128)}) %all-reduce.5.cloned.1.call-update) | async-done | bytes 131088 | tf_op jit(solution)/shard_map/psum | solution.py:56
  366.1 0.8 fusion.6
  366.9 0.9 multiply_reduce_fusion.1
  367.8 158.4 %all-reduce = (f32[16,256]{1,0:T(8,128)S(1)}, f32[256]{0:T(256)S(1)}, f32[16]{0:T(128)S(1)}) all-reduce(f32[16,256]{1,0:T(8,128)S(1)} %fusion.6, f32[256]{0:T(256)S(1)} %multiply_reduce_fusion, f32[16]{0:T(128)S(1)} %multiply_reduce_fusion.1), channel_id=1, replica_groups=mesh['dp'=32,'tensor'=16] {'dp'}, use_global_device_ids=true, to_apply=%region_3.0 | all-reduce | flops 4368 | bytes 34944 | tf_op jit(solution)/shard_map/psum | solution.py:64
  526.2 0.7 multiply_multiply_fusion
  (3 shorter events, 0.0 us)
Async XLA Ops:
  6.5 236.5 %copy-start = (bf16[8192,128]{1,0:T(8,128)(2,1)S(1)}, bf16[8192,128]{1,0:T(8,128)(2,1)}, u32[]{:S(2)}) copy-start(bf16[8192,128]{1,0:T(8,128)(2,1)} %param.12) | copy-start | bytes 6291460
  6.5 124.0 %all-reduce.7.cloned.1.call-start = ((), (), s32[]{:S(2)}) async-start(), calls=%async_computation.2 | async-start | bytes 131072 | tf_op jit(solution)/shard_map/psum | solution.py:38
  11.2 231.9 %all-gather.2.cloned.1.call-start = ((), (), s32[]{:S(2)}) async-start(), calls=%async_computation | async-start | bytes 4325376 | tf_op jit(solution)/shard_map/all_gather | solution.py:52
  134.0 113.2 %copy-start.1 = (bf16[256,128]{1,0:T(8,128)(2,1)S(1)}, bf16[256,128]{1,0:T(8,128)(2,1)}, u32[]{:S(2)}) copy-start(bf16[256,128]{1,0:T(8,128)(2,1)} %param.13) | copy-start | bytes 196612
  136.4 229.6 %all-reduce.5.cloned.1.call-start = ((), (), s32[]{:S(2)}) async-start(), calls=%async_computation.1 | async-start | bytes 262144 | tf_op jit(solution)/shard_map/psum | solution.py:56
Sparse Core Ops, SparseCore 0:
  11.3 119.1 all-reduce.6
  136.6 106.4 all-gather.1
  247.3 118.7 all-reduce.4
where the time goes:
time: 536 us; the launch traced here: 533 us
  waiting for transfers between devices  344 us (64%)
  blocking collectives  158 us (29%)
  between operations  13.2 us (2%)
  matrix products  12.5 us (2%)
    psum x1, blocking collectives, body(): inner, train_sq, target_sq = lax.psum((inner, train_sq, target_sq), 'dp')  158 us
    psum x1, waiting for transfers between devices, body(): summed = lax.psum(partial_sum, 'tensor')  119 us
    psum x1, waiting for transfers between devices, body(): lax.psum((down_part, up_portion), 'tensor')  119 us
    all_gather x1, waiting for transfers between devices, body(): lax.all_gather(gradients, 'dp', axis=0, tiled=True)  107 us
  transfers between devices with their start and end apart: 3, of which 3 were waited for; matrix products, arithmetic and copies ran while one was open for 0% of the time, Pallas kernels for 0%

commit v1 on v0

v1 whole, which is shorter than its diff:
```python
import heapq
import math

import jax
import jax.numpy as jnp
from jax import lax
from jax.experimental import pallas as pl
from jax.experimental.pallas import tpu as pltpu
from jax.sharding import PartitionSpec as P

MESH = pl.DeviceIdType.MESH
K = 4096
SCALE = 2.0
EPS = 1e-06
NZ, NY, NT = 8, 4, 16
NA = 5
NB = 8 - NA
WA, WB = NA * 512, NB * 512
HALF = (NA * 512 // 256) * 128
PLUS = {0: 4, 1: 3, 2: 4, 3: 3}
F32, BF16 = jnp.float32, jnp.bfloat16


def hops(r, way):
    return PLUS[r] if way == "+" else 7 - PLUS[r]


def follow(tag, halves):
    kind = tag[0]
    ta, tb = NA * 0.328, NB * 0.328

    def along_z(r):
        return [("z+", ("Az", r, "+", 1), ta), ("z-", ("Az", r, "-", 1), ta)]

    def along_y(o):
        return [("y+", ("By", "+", o), 2 * tb), ("y-", ("By", "-", o), 2 * tb)]

    if kind == "own":
        first = [("y+", ("Ay", 3), 2 * ta), ("y-", ("Ay", 1), 2 * ta)]
        first += [("z+", ("Bz", "+", 1), tb), ("z-", ("Bz", "-", 1), tb)]
        return first + along_z(0) + along_y(0)
    if kind == "Ay":
        if tag[1] == 3:
            return [("y+", ("Ay", "2a"), ta)] + along_z(3)
        if tag[1] == 1:
            return [("y-", ("Ay", "2b"), ta)] + along_z(1)
        halves.append(tag)
        return along_z(2) if len(halves) == 2 else []
    if kind == "Az":
        _, r, way, h = tag
        return [("z" + way, ("Az", r, way, h + 1), ta)] if h < hops(r, way) else []
    if kind == "Bz":
        _, way, h = tag
        on = [("z" + way, ("Bz", way, h + 1), tb)] if h < (4 if way == "+" else 3) else []
        return on + along_y(-h if way == "+" else h)
    if kind == "By":
        _, way, o = tag
        return [("y" + way, ("Bo", way, o), 2 * tb)] if (o % 2 == 0) == (way == "+") else []
    return []


def plan():
    free = dict.fromkeys(("z+", "z-", "y+", "y-"), 0.0)
    heap, order, halves, count = [(0.0, 0, ("own",))], [], [], 0
    while heap:
        now, _, tag = heapq.heappop(heap)
        sends = follow(tag, halves)
        order.append((tag, [(link, new) for link, new, _ in sends]))
        for link, new, length in sends:
            count += 1
            free[link] = max(now, free[link]) + length
            heapq.heappush(heap, (free[link] + 1.5, count, new))
    return order


ORDER = plan()
TAGS = [tag for tag, _ in ORDER[1:]]
TAGS += [(k, r) for k in ("h", "f", "p") for r in range(1, NT)]
TAGS += [(k, r) for k in ("y1", "y2", "ty") for r in range(1, NY)]
TAGS += [(k, r) for k in ("z1", "tz") for r in range(1, NZ)]
INDEX = {tag: i for i, tag in enumerate(TAGS)}


def kernel(
    act_in, cot_in, lengths, down, up, proj_in, target, out,
    act, cot, proj, pc, ga, gb, hid, hrecv, facs, parta, partb, sbuf, precv,
    tq, tqy, tqz, y1s, y1r, z1r, fin, lsem, ssem, rsem,
):
    dp, me = lax.axis_index("dp"), lax.axis_index("tensor")
    z, y = lax.div(dp, NY), lax.rem(dp, NY)

    def at_z(o):
        return lax.rem(z + (o % NZ), NZ)

    def at_y(o):
        return lax.rem(y + (o % NY), NY)

    def at_t(o):
        return lax.rem(me + (o % NT), NT)

    def dev(zz, yy):
        return (zz * NY + yy, me)

    def copy(tag, src, dst, device):
        i = INDEX[tag]
        return pltpu.make_async_remote_copy(
            src_ref=src, dst_ref=dst, send_sem=ssem.at[i], recv_sem=rsem.at[i],
            device_id=device, device_id_type=MESH,
        )

    sent = []

    def send(tag, src, dst, device):
        c = copy(tag, src, dst, device)
        c.start()
        sent.append(c)

    def wait(tag, ref):
        copy(tag, ref, ref, dev(at_z(1), y)).wait_recv()

    loads = [
        pltpu.make_async_copy(a, b, lsem.at[i])
        for i, (a, b) in enumerate(((act_in, act), (cot_in, cot), (proj_in, proj)))
    ]
    for c in loads:
        c.start()

    barrier = pltpu.get_barrier_semaphore()
    partners = [(dp, at_t(r)) for r in range(1, NT)]
    partners += [dev(at_z(o), y) for o in range(1, NZ)] + [dev(z, at_y(o)) for o in range(1, NY)]
    for p in partners:
        pl.semaphore_signal(barrier, inc=1, device_id=p, device_id_type=MESH)

    nt = (((1,), (1,)), ((), ()))
    loads[0].wait()
    for e in range(8):
        hid[8 + e] = lax.dot_general(down[...], act[e], nt, preferred_element_type=F32)
    loads[1].wait()
    for e in range(8):
        hid[e] = lax.dot_general(up[...], cot[e], nt, preferred_element_type=F32)
    pl.semaphore_wait(barrier, len(partners))
    for r in range(1, NT):
        p = at_t(r)
        send(("h", r), hid.at[p], hrecv.at[me], (dp, p))
    hrecv[me] = hid[me]

    rows = target[...].astype(F32)
    ones = jnp.ones((8, 128), F32)
    norms = lax.dot_general(
        ones, rows * rows, nt, precision=lax.Precision.HIGHEST, preferred_element_type=F32
    )
    which = lax.broadcasted_iota(jnp.int32, (8, 128), 0)
    tq[...] = jnp.where(which == 0, norms[:, :128], norms[:, 128:])
    for r in range(1, NY):
        send(("ty", r), tq, tqy.at[y], dev(z, at_y(r)))
    tqy[y] = tq[...]

    q = lax.broadcasted_iota(jnp.int32, (256, 256), 0)
    c = lax.broadcasted_iota(jnp.int32, (256, 256), 1)
    swap = jnp.where(c == lax.rem(q, 16) * 16 + lax.div(q, 16), 1.0, 0.0).astype(BF16)

    def turn(b, carry):
        block = proj[pl.ds(pl.multiple_of(b * 256, 256), 256), :]
        moved = jnp.dot(swap, block, preferred_element_type=F32).astype(BF16)
        for j in range(16):
            at = pl.ds(pl.multiple_of(b * 16 + (j % 8) * 512, 16), 16)
            pc[at, (j // 8) * 128 : (j // 8) * 128 + 128] = moved[j * 16 : j * 16 + 16]
        return carry

    loads[2].wait()
    lax.fori_loop(0, 16, turn, 0)

    for r in range(1, NT):
        wait(("h", r), hrecv.at[at_t(-r)])
    total = hrecv[0]
    for t in range(1, NT):
        total = total + hrecv[t]
    token = lax.broadcasted_iota(jnp.int32, (8, 128), 1)
    facs[me] = jnp.where(token < lengths[lax.rem(me, 8)], SCALE, 0.0) * total
    for r in range(1, NT):
        send(("f", r), facs.at[me], facs.at[me], (dp, at_t(r)))

    for r in range(1, NY):
        wait(("ty", r), tqy.at[at_y(-r)])
    tqz[z] = (tqy[0] + tqy[1]) + (tqy[2] + tqy[3])
    for r in range(1, NZ):
        send(("tz", r), tqz.at[z], tqz.at[z], dev(at_z(r), y))
    lax.fori_loop(16, 32, turn, 0)

    for r in range(1, NT):
        wait(("f", r), facs.at[at_t(-r)])
    own = lax.broadcasted_iota(jnp.int32, (8, 8, 128), 1)
    grads = []
    for a, data in ((0, act), (1, cot)):
        parts = []
        for e in range(8):
            spread = jnp.broadcast_to(facs[a * 8 + e][:, None, :], (8, 8, 128))
            parts.append(jnp.where(own == e, spread, 0.0).reshape(64, 128).astype(BF16))
        left = jnp.concatenate(parts, axis=1)
        grads.append(jnp.dot(left, data[...].reshape(1024, 512), preferred_element_type=F32))
    for j in range(8):
        tile = jnp.concatenate([g[j * 8 : j * 8 + 8] for g in grads], axis=0).astype(BF16)
        if j < NA:
            ga[dp, :, j * 512 : j * 512 + 512] = tile
        else:
            gb[y * NZ + z, :, (j - NA) * 512 : (j - NA) * 512 + 512] = tile

    def slot(tag):
        kind = tag[0]
        if kind == "Ay":
            if tag[1] in (1, 3):
                return ga.at[z * NY + at_y(tag[1])]
            lanes = pl.ds(0, HALF) if tag[1] == "2a" else pl.ds(HALF, WA - HALF)
            return ga.at[z * NY + at_y(2), :, lanes]
        if kind == "Az":
            _, r, way, h = tag
            return ga.at[at_z(-h if way == "+" else h) * NY + at_y(r)]
        if kind == "Bz":
            _, way, h = tag
            return gb.at[y * NZ + at_z(-h if way == "+" else h)]
        _, way, o = tag
        r = 2 if kind == "Bo" else (-1 if way == "+" else 1)
        return gb.at[at_y(r) * NZ + at_z(o)]

    def source(link, new):
        kind = new[0]
        s = 1 if link[1] == "+" else -1
        if kind == "Ay":
            if new[1] in (1, 3):
                return ga.at[dp]
            lanes = pl.ds(0, HALF) if new[1] == "2a" else pl.ds(HALF, WA - HALF)
            return ga.at[z * NY + at_y(-s), :, lanes]
        if kind == "Az":
            _, r, _, h = new
            return ga.at[at_z(-s * (h - 1)) * NY + at_y(r)]
        if kind == "Bz":
            return gb.at[y * NZ + at_z(-s * (new[2] - 1))]
        o = new[2]
        return gb.at[(y if kind == "By" else at_y(-s)) * NZ + at_z(o)]

    def fold(found):
        found = found.reshape(-1, 2, 8, 256)
        return found[:, 0, :, :128] + found[:, 1, :, 128:]

    def product_a(o):
        first = at_z(o) * NY
        block = ga[pl.ds(first, NY)].reshape(NY * 16, WA)
        parta[pl.ds(first, NY)] = fold(jnp.dot(block, pc[:WA, :], preferred_element_type=F32))

    def product_b(r):
        first = at_y(r) * NZ
        block = gb[pl.ds(first, NZ)].reshape(NZ * 16, WB)
        partb[pl.ds(first, NZ)] = fold(jnp.dot(block, pc[WA:, :], preferred_element_type=F32))

    need_a = {o: 4 for o in range(NZ)}
    need_b = {r: 8 for r in range(NY)}
    for tag, sends in ORDER:
        if tag != ("own",):
            wait(tag, slot(tag))
        for link, new in sends:
            step = 1 if link[1] == "+" else -1
            to = dev(at_z(step), y) if link[0] == "z" else dev(z, at_y(step))
            ref = source(link, new)
            send(new, ref, ref, to)
        kind = tag[0]
        if kind == "own":
            need_a[0] -= 1
            need_b[0] -= 1
        elif kind == "Ay":
            need_a[0] -= 1 if tag[1] in (1, 3) else 0.5
            if need_a[0] == 0:
                product_a(0)
        elif kind == "Az":
            o = (-tag[3] if tag[2] == "+" else tag[3]) % NZ
            need_a[o] -= 1
            if need_a[o] == 0:
                product_a(o)
        else:
            r = 0 if kind == "Bz" else 2 if kind == "Bo" else 3 if tag[1] == "+" else 1
            need_b[r] -= 1
            if need_b[r] == 0:
                product_b(r)
    assert not any(need_a.values()) and not any(need_b.values())

    for p in range(NT):
        pair = []
        for d in (2 * p, 2 * p + 1):
            pair.append(parta[d] + partb[(d % NY) * NZ + d // NY])
        sbuf[p] = jnp.concatenate(pair, axis=0)
    for r in range(1, NT):
        p = at_t(r)
        send(("p", r), sbuf.at[p], precv.at[me], (dp, p))
    precv[me] = sbuf[me]
    for r in range(1, NT):
        wait(("p", r), precv.at[at_t(-r)])
    projected = precv[0]
    for t in range(1, NT):
        projected = projected + precv[t]

    inner = lax.dot_general(
        projected, rows, nt, precision=lax.Precision.HIGHEST, preferred_element_type=F32
    )
    square = jnp.broadcast_to(jnp.sum(projected * projected, axis=1, keepdims=True), (16, 128))
    for i in range(NY):
        up_rows, lanes = slice((i // 2) * 8, (i // 2) * 8 + 8), slice((i % 2) * 128, (i % 2) * 128 + 128)
        y1s[i, 0] = inner[up_rows, lanes]
        y1s[i, 1] = square[up_rows, :]
    for r in range(1, NY):
        send(("y1", r), y1s.at[at_y(r)], y1r.at[y], dev(z, at_y(r)))
    y1r[y] = y1s[y]
    for r in range(1, NY):
        wait(("y1", r), y1r.at[at_y(-r)])
    z1r[z] = (y1r[0] + y1r[1]) + (y1r[2] + y1r[3])
    for r in range(1, NZ):
        send(("z1", r), z1r.at[z], z1r.at[z], dev(at_z(r), y))
    for r in range(1, NZ):
        wait(("tz", r), tqz.at[at_z(-r)])
    norm = tqz[0]
    for t in range(1, NZ):
        norm = norm + tqz[t]
    norm = jnp.where(lax.rem(y, 2) == 0, norm[0:1], norm[1:2])
    for r in range(1, NZ):
        wait(("z1", r), z1r.at[at_z(-r)])
    both = z1r[0]
    for t in range(1, NZ):
        both = both + z1r[t]
    fin[y] = math.sqrt(K) * both[0] * lax.rsqrt(both[1] + EPS) * lax.rsqrt(norm + EPS)
    for r in range(1, NY):
        send(("y2", r), fin.at[y], fin.at[y], dev(z, at_y(r)))
    for r in range(1, NY):
        wait(("y2", r), fin.at[at_y(-r)])
    for i in range(NY):
        out[(i // 2) * 8 : (i // 2) * 8 + 8, (i % 2) * 128 : (i % 2) * 128 + 128] = fin[i]
    for c in sent:
        c.wait_send()


def body(activations, cotangents, lengths, down, up, projection, target):
    vmem, hbm = pl.BlockSpec(memory_space=pltpu.VMEM), pl.BlockSpec(memory_space=pl.ANY)
    smem = pl.BlockSpec(memory_space=pltpu.SMEM)
    return pl.pallas_call(
        kernel,
        out_shape=jax.ShapeDtypeStruct((16, 256), F32),
        in_specs=[hbm, hbm, smem, vmem, vmem, hbm, vmem],
        out_specs=vmem,
        scratch_shapes=[
            pltpu.VMEM((8, 128, 512), BF16),
            pltpu.VMEM((8, 128, 512), BF16),
            pltpu.VMEM((8192, 128), BF16),
            pltpu.VMEM((4096, 256), BF16),
            pltpu.VMEM((32, 16, WA), BF16),
            pltpu.VMEM((32, 16, WB), BF16),
            pltpu.VMEM((16, 8, 128), F32),
            pltpu.VMEM((16, 8, 128), F32),
            pltpu.VMEM((16, 8, 128), F32),
            pltpu.VMEM((32, 8, 128), F32),
            pltpu.VMEM((32, 8, 128), F32),
            pltpu.VMEM((16, 16, 128), F32),
            pltpu.VMEM((16, 16, 128), F32),
            pltpu.VMEM((8, 128), F32),
            pltpu.VMEM((4, 8, 128), F32),
            pltpu.VMEM((8, 8, 128), F32),
            pltpu.VMEM((4, 2, 8, 128), F32),
            pltpu.VMEM((4, 2, 8, 128), F32),
            pltpu.VMEM((8, 2, 8, 128), F32),
            pltpu.VMEM((4, 8, 128), F32),
            pltpu.SemaphoreType.DMA((3,)),
            pltpu.SemaphoreType.DMA((len(TAGS),)),
            pltpu.SemaphoreType.DMA((len(TAGS),)),
        ],
        compiler_params=pltpu.CompilerParams(
            collective_id=0, has_side_effects=True, vmem_limit_bytes=40 * 1024 * 1024
        ),
    )(activations, cotangents, lengths, down.T, up, projection, target)


def solution(mesh):
    placed = (
        P("dp", None, "tensor"),
        P("dp", None, "tensor"),
        P("dp"),
        P("tensor", None),
        P(None, "tensor"),
        P("tensor", "dp"),
        P(None, "dp"),
    )
    return jax.shard_map(
        body, mesh=mesh, in_specs=placed, out_specs=P("tensor", None), check_vma=False
    )
```

time: 536 us -> 92.3 us (0.17)
  waiting for transfers between devices: 344 us -> 0 us
  blocking collectives: 158 us -> 0 us
  Pallas kernels: 0 us -> 83.3 us
  between operations: 13.2 us -> 0.02 us
  matrix products: 12.5 us -> 0 us
    psum x2 -> x0, waiting for transfers between devices: 237 us -> none  [the longest x1 119 us: body(): summed = lax.psum(partial_sum, 'tensor')]
    psum x1 -> x0, blocking collectives: 158 us -> none  [body(): inner, train_sq, target_sq = lax.psum((inner, train_sq, target_sq), 'dp')]
    all_gather x1 -> x0, waiting for transfers between devices: 107 us -> none  [body(): lax.all_gather(gradients, 'dp', axis=0, tiled=True)]
    pallas_call x0 -> x1, Pallas kernels: none -> 83.3 us  [body(): pl.pallas_call(kernel, out_shape=jax.ShapeDtypeStruct((16, 256), F32), in...]
    dot_general x6 -> x0, matrix products: 12.5 us -> none  [the longest x1 4.07 us: body(): jnp.dot(lax.all_gather(gradients, 'dp', axis=0, tiled=True), projection,...]
    unnamed x4 -> x15, local copies, waits for them, and re-layouts: 0.01 us -> 7.53 us
  transfers between devices with their start and end apart: 3 -> 0, of which waited for: 3 -> 0; matrix products, arithmetic and copies ran while one was open for 0% -> 0% of each run, Pallas kernels for 0% -> 0%
where the time goes in v1:
time: 92.3 us; the launch traced here: 90.8 us
  Pallas kernels  83.3 us (90%)
  local copies, waits for them, and re-layouts  7.53 us (8%)
    pallas_call x1, Pallas kernels, body(): pl.pallas_call(kernel, out_shape=jax.ShapeDtypeStruct((16, 256), F32), in...  83.3 us
    unnamed x15, local copies, waits for them, and re-layouts  7.53 us

profile of v1, /device:TPU:6, one launch (start us, length us, event | category | flops | bytes accessed | tf_op | source)
XLA Modules:
  0.0 90.8 jit_solution(13560464190496606054)
XLA Ops:
  0.0 0.0 copy-start
  0.0 1.6 %copy-done = bf16[8192,128]{1,0:T(8,128)(2,1)S(1)} copy-done((bf16[8192,128]{1,0:T(8,128)(2,1)S(1)}, bf16[8192,128]{1,0:T(8,128)(2,1)}, u32[]{:S(2)}) %copy-start) | copy-done | bytes 2097176
  1.6 0.0 copy-start.1
  1.6 1.2 %copy-done.1 = bf16[8,128,512]{2,1,0:T(8,128)(2,1)S(1)} copy-done((bf16[8,128,512]{2,1,0:T(8,128)(2,1)S(1)}, bf16[8,128,512]{2,1,0:T(8,128)(2,1)}, u32[]{:S(2)}) %copy-start.1) | copy-done | bytes 1048600
  2.8 0.0 copy-start.2
  2.8 1.2 %copy-done.2 = bf16[8,128,512]{2,1,0:T(8,128)(2,1)S(1)} copy-done((bf16[8,128,512]{2,1,0:T(8,128)(2,1)S(1)}, bf16[8,128,512]{2,1,0:T(8,128)(2,1)}, u32[]{:S(2)}) %copy-start.2) | copy-done | bytes 1048600
  4.0 0.0 copy-start.3
  4.0 0.8 copy-done.3
  4.9 0.0 copy-start.4
  4.9 0.7 copy-done.4
  5.6 0.0 copy-start.5
  5.6 0.7 copy-done.5
  6.3 0.0 copy-start.6
  6.3 0.7 copy-done.6
  6.9 83.3 %shard_map.73 = f32[16,256]{1,0:T(8,128)S(1)} custom-call(bf16[8,128,512]{2,1,0:T(8,128)(2,1)S(1)} %copy-done.1, bf16[8,128,512]{2,1,0:T(8,128)(2,1)S(1)} %copy-done.2, s32[8]{0:T(128)S(1)} %copy-done.6, bf16[8,512]{1,0:T(8,128)(2,1)S(1)} %bitcast.1, bf16[8,512]{1,0:T(8,128)(2,1)S(1)} %copy-done.5, bf16[8192,128]{1,0:T(8,128)(2,1)S(1)} %copy-done, ...), custom_call_target="tpu_custom_call" | custom-call | tf_op jit(solution)/shard_map/pallas_call | solution.py:341
  90.2 0.6 copy.9
Async XLA Ops:
  0.0 1.6 %copy-start = (bf16[8192,128]{1,0:T(8,128)(2,1)S(1)}, bf16[8192,128]{1,0:T(8,128)(2,1)}, u32[]{:S(2)}) copy-start(bf16[8192,128]{1,0:T(8,128)(2,1)} %proj_in.1) | copy-start | bytes 6291460
  1.6 1.2 %copy-start.1 = (bf16[8,128,512]{2,1,0:T(8,128)(2,1)S(1)}, bf16[8,128,512]{2,1,0:T(8,128)(2,1)}, u32[]{:S(2)}) copy-start(bf16[8,128,512]{2,1,0:T(8,128)(2,1)} %act_in.1) | copy-start | bytes 3145732
  2.8 1.2 %copy-start.2 = (bf16[8,128,512]{2,1,0:T(8,128)(2,1)S(1)}, bf16[8,128,512]{2,1,0:T(8,128)(2,1)}, u32[]{:S(2)}) copy-start(bf16[8,128,512]{2,1,0:T(8,128)(2,1)} %cot_in.1) | copy-start | bytes 3145732
  4.0 0.8 copy-start.3
  4.9 0.7 copy-start.4
  5.6 0.7 copy-start.5
  6.3 0.7 copy-start.6

commit v2 on v1

v2 whole, which is shorter than its diff:
```python
import heapq
import math

import jax
import jax.numpy as jnp
from jax import lax
from jax.experimental import pallas as pl
from jax.experimental.pallas import tpu as pltpu
from jax.sharding import PartitionSpec as P

MESH = pl.DeviceIdType.MESH
K = 4096
SCALE = 2.0
EPS = 1e-06
NZ, NY, NT = 8, 4, 16
W = 1024
F32, BF16 = jnp.float32, jnp.bfloat16


def onward(o, r):
    if o in (-1, 1):
        return [(3 * o, "z+" if o < 0 else "z-")]
    if o in (-2, 2) and (o < 0) == (r % 2 == 0):
        return [(4, "z+" if o < 0 else "z-")]
    return []


def follow(tag):
    kind = tag[0]
    if kind == "own":
        sends = [("y" + w, ("Ay", c, 3 if w == "+" else 1), 2) for c in "so" for w in "+-"]
        for o, links in ((1, 1), (2, 2)):
            sends += [("z+", ("Bz", -o), links), ("z-", ("Bz", o), links)]
        for o, links in ((1, 1), (2, 2)):
            sends += [("z+", ("Az", 0, -o), links), ("z-", ("Az", 0, o), links)]
        return sends + [("y+", ("By", "+", 0), 2), ("y-", ("By", "-", 0), 2)]
    if kind == "Ay":
        _, c, r = tag
        o = 2 if c == "s" else 1
        sends = [("z+", ("Az", r, -o), o), ("z-", ("Az", r, o), o)]
        if (c, r) in (("s", 3), ("o", 1)):
            sends = [("y+" if c == "s" else "y-", ("Ay", c, 2), 2)] + sends
        return sends
    if kind == "Az":
        return [(link, ("Az", tag[1], o), 2) for o, link in onward(tag[2], tag[1])]
    if kind == "Bz":
        on = [(link, ("Bz", o), 2) for o, link in onward(tag[1], 0)]
        return on + [("y+", ("By", "+", tag[1]), 2), ("y-", ("By", "-", tag[1]), 2)]
    if kind == "By" and (tag[2] % 2 == 0) == (tag[1] == "+"):
        return [("y" + tag[1], ("Bo", tag[1], tag[2]), 2)]
    return []


def plan():
    free = dict.fromkeys(("z+", "z-", "y+", "y-"), 0.0)
    heap, order, count = [(0.0, 0, ("own",))], [], 0
    while heap:
        now, _, tag = heapq.heappop(heap)
        sends = follow(tag)
        order.append((now, tag, [(link, new) for link, new, _ in sends]))
        for link, new, links in sends:
            count += 1
            free[link] = max(now, free[link]) + links * 0.655
            heapq.heappush(heap, (free[link] + 2.2 + 0.6 * links, count, new))
    return order


ORDER = [(tag, sends) for _, tag, sends in plan()]
TAGS = [tag for tag, _ in ORDER[1:]]
TAGS += [(k, r) for k in ("h", "f", "p") for r in range(1, NT)]
TAGS += [(k, r) for k in ("y1", "y2", "ty") for r in range(1, NY)]
TAGS += [(k, r) for k in ("z1", "tz") for r in range(1, NZ)]
TAGS += [("pu",), ("pd",)] + [("ra", o) for o in range(NZ)] + [("rb", r) for r in range(NY)]
INDEX = {tag: i for i, tag in enumerate(TAGS)}


def kernel(
    act_in, cot_in, lengths_in, down_in, up_in, proj_in, target_in, out,
    act, cot, lengths, down, up, proj, target, pc, neighbours, own_blocks, other, ga, gb, hid, hrecv, facs, pa, pb,
    sbuf, precv,
    tq, tqy, tqz, y1s, y1r, z1r, fin, lsem, ssem, rsem,
):
    dp, me = lax.axis_index("dp"), lax.axis_index("tensor")
    z, y = lax.div(dp, NY), lax.rem(dp, NY)
    parity = lax.rem(z, 2)

    def at_z(o):
        return lax.rem(z + (o % NZ), NZ)

    def at_y(o):
        return lax.rem(y + (o % NY), NY)

    def at_t(o):
        return lax.rem(me + (o % NT), NT)

    def dev(zz, yy):
        return (zz * NY + yy, me)

    def copy(tag, src, dst, device):
        i = INDEX[tag]
        return pltpu.make_async_remote_copy(
            src_ref=src, dst_ref=dst, send_sem=ssem.at[i], recv_sem=rsem.at[i],
            device_id=device, device_id_type=MESH,
        )

    sent = []

    def send(tag, src, dst, device):
        c = copy(tag, src, dst, device)
        c.start()
        sent.append(c)

    def wait(tag, ref):
        copy(tag, ref, ref, dev(at_z(1), y)).wait_recv()

    ends = (
        (down_in, down), (act_in, act), (up_in, up), (cot_in, cot),
        (target_in, target), (lengths_in, lengths), (proj_in, proj),
    )
    loads = [pltpu.make_async_copy(a, b, lsem.at[i]) for i, (a, b) in enumerate(ends)]
    for c in loads:
        c.start()

    barrier = pltpu.get_barrier_semaphore()
    partners = [(dp, at_t(r)) for r in range(1, NT)]
    partners += [dev(at_z(o), y) for o in range(1, NZ)] + [dev(z, at_y(o)) for o in range(1, NY)]
    for p in partners:
        pl.semaphore_signal(barrier, inc=1, device_id=p, device_id_type=MESH)

    nt = (((1,), (1,)), ((), ()))
    loads[0].wait()
    loads[1].wait()
    for e in range(8):
        hid[8 + e] = lax.dot_general(down[...], act[e], nt, preferred_element_type=F32)
    loads[2].wait()
    loads[3].wait()
    for e in range(8):
        hid[e] = lax.dot_general(up[...], cot[e], nt, preferred_element_type=F32)
    pl.semaphore_wait(barrier, len(partners))
    loads[6].wait()
    theirs = pl.multiple_of((1 - parity) * 4096, 4096)
    for r in range(1, NT):
        p = at_t(r)
        send(("h", r), hid.at[p], hrecv.at[me], (dp, p))
    send(("pu",), proj.at[pl.ds(theirs, 2048)], neighbours.at[0], dev(at_z(-1), y))
    send(("pd",), proj.at[pl.ds(theirs + 2048, 2048)], neighbours.at[1], dev(at_z(1), y))
    hrecv[me] = hid[me]

    loads[4].wait()
    rows = target[...].astype(F32)
    ones = jnp.ones((8, 128), F32)
    norms = lax.dot_general(
        ones, rows * rows, nt, precision=lax.Precision.HIGHEST, preferred_element_type=F32
    )
    which = lax.broadcasted_iota(jnp.int32, (8, 128), 0)
    tq[...] = jnp.where(which == 0, norms[:, :128], norms[:, 128:])
    for r in range(1, NY):
        send(("ty", r), tq, tqy.at[y], dev(z, at_y(r)))
    tqy[y] = tq[...]

    q = lax.broadcasted_iota(jnp.int32, (256, 256), 0)
    c = lax.broadcasted_iota(jnp.int32, (256, 256), 1)
    swap = jnp.where(c == lax.rem(q, 16) * 16 + lax.div(q, 16), 1.0, 0.0).astype(BF16)

    def turn(source, first, to):
        def step(b, carry):
            block = source[pl.ds(pl.multiple_of(first + b * 256, 256), 256), :]
            moved = jnp.dot(swap, block, preferred_element_type=F32).astype(BF16)
            for j in range(16):
                at = pl.ds(pl.multiple_of(b * 16 + (j % 8) * 128, 16), 16)
                to[at, (j // 8) * 128 : (j // 8) * 128 + 128] = moved[j * 16 : j * 16 + 16]
            return carry

        lax.fori_loop(0, 8, step, 0, unroll=True)

    mine = pl.multiple_of(parity * 4096, 4096)
    turn(proj, mine, pc.at[0])
    turn(proj, mine + 2048, pc.at[1])

    for r in range(1, NT):
        wait(("h", r), hrecv.at[at_t(-r)])
    total = hrecv[0]
    for t in range(1, NT):
        total = total + hrecv[t]
    loads[5].wait()
    token = lax.broadcasted_iota(jnp.int32, (8, 128), 1)
    facs[me] = jnp.where(token < lengths[lax.rem(me, 8)], SCALE, 0.0) * total
    for r in range(1, NT):
        send(("f", r), facs.at[me], facs.at[me], (dp, at_t(r)))

    for r in range(1, NY):
        wait(("ty", r), tqy.at[at_y(-r)])
    tqz[z] = (tqy[0] + tqy[1]) + (tqy[2] + tqy[3])
    for r in range(1, NZ):
        send(("tz", r), tqz.at[z], tqz.at[z], dev(at_z(r), y))

    for r in range(1, NT):
        wait(("f", r), facs.at[at_t(-r)])
    own = lax.broadcasted_iota(jnp.int32, (8, 8, 128), 1)
    grads = []
    for a, data in ((0, act), (1, cot)):
        parts = []
        for e in range(8):
            spread = jnp.broadcast_to(facs[a * 8 + e][:, None, :], (8, 8, 128))
            parts.append(jnp.where(own == e, spread, 0.0).reshape(64, 128).astype(BF16))
        left = jnp.concatenate(parts, axis=1)
        grads.append(jnp.dot(left, data[...].reshape(1024, 512), preferred_element_type=F32))
    for j in range(8):
        tile = jnp.concatenate([g[j * 8 : j * 8 + 8] for g in grads], axis=0).astype(BF16)
        for i in range(4):
            own_blocks[i, :, j * 128 : j * 128 + 128] = tile[:, i * 128 : i * 128 + 128]
    same, not_same = 2 * parity, 2 - 2 * parity
    ga[dp] = own_blocks[same]
    gb[y * NZ + z] = own_blocks[same + 1]

    def slot_a(o, r):
        return ga.at[at_z(o) * NY + at_y(r)]

    def slot_b(o, r):
        return gb.at[at_y(r) * NZ + at_z(o)]

    def slot(tag):
        kind = tag[0]
        if kind == "Ay":
            return slot_a(0, tag[2]) if tag[1] == "s" else other.at[tag[2] - 1]
        if kind == "Az":
            return slot_a(tag[2], tag[1])
        if kind == "Bz":
            return slot_b(tag[1], 0)
        return slot_b(tag[2], 2 if kind == "Bo" else 3 if tag[1] == "+" else 1)

    def ends_of(link, new):
        kind = new[0]
        s = 1 if link[1] == "+" else -1
        if kind == "Ay":
            _, c, r = new
            if c == "s":
                ref = slot_a(0, 0 if r != 2 else -s)
                return ref, ref
            here = own_blocks.at[not_same] if r != 2 else other.at[(-s) % NY - 1]
            return here, other.at[r - 1]
        if kind in ("Az", "Bz"):
            o, r = new[-1], new[1] if kind == "Az" else 0
            place = slot_a if kind == "Az" else slot_b
            if abs(o) == 1:
                there = place(0, r)
                if kind == "Bz":
                    return own_blocks.at[not_same + 1], there
                return (own_blocks.at[not_same] if r == 0 else other.at[r - 1]), there
            ref = place(0 if abs(o) == 2 else -s * (abs(o) - 2), r)
            return ref, ref
        ref = slot_b(new[2], 0 if kind == "By" else -s)
        return ref, ref

    def fold(found):
        found = found.reshape(-1, 2, 8, 256)
        return found[:, 0, :, :128] + found[:, 1, :, 128:]

    def product_a(o):
        at = pl.ds(at_z(o) * NY, NY)
        block = ga[at].reshape(NY * 16, W)
        pa[1, at] = fold(jnp.dot(block, pc[2], preferred_element_type=F32))
        send(("ra", o), pa.at[1, at], pa.at[2, at], dev(at_z(1), y))
        pa[0, at] = fold(jnp.dot(block, pc[0], preferred_element_type=F32))

    def product_b(r):
        at = pl.ds(at_y(r) * NZ, NZ)
        block = gb[at].reshape(NZ * 16, W)
        pb[1, at] = fold(jnp.dot(block, pc[3], preferred_element_type=F32))
        send(("rb", r), pb.at[1, at], pb.at[2, at], dev(at_z(-1), y))
        pb[0, at] = fold(jnp.dot(block, pc[1], preferred_element_type=F32))

    come = []

    def products(run, which):
        if not come:
            wait(("pu",), neighbours.at[0])
            turn(neighbours.at[0], 0, pc.at[2])
            wait(("pd",), neighbours.at[1])
            turn(neighbours.at[1], 0, pc.at[3])
        come.append(run)
        run(which)

    need_a = {o: 4 for o in range(NZ)}
    need_b = {r: 8 for r in range(NY)}
    for tag, sends in ORDER:
        if tag != ("own",):
            wait(tag, slot(tag))
        for link, new in sends:
            links = 1 if link[0] == "y" or abs(new[-1]) == 1 else 2
            step = links if link[1] == "+" else -links
            to = dev(at_z(step), y) if link[0] == "z" else dev(z, at_y(step))
            send(new, *ends_of(link, new), to)
        kind = tag[0]
        if kind in ("own", "Ay", "Az") and tag[1:2] != ("o",):
            o = tag[2] % NZ if kind == "Az" else 0
            need_a[o] -= 1
            if need_a[o] == 0:
                products(product_a, o)
        if kind in ("own", "Bz", "By", "Bo"):
            r = 2 if kind == "Bo" else 0 if kind != "By" else 3 if tag[1] == "+" else 1
            need_b[r] -= 1
            if need_b[r] == 0:
                products(product_b, r)
    assert not any(need_a.values()) and not any(need_b.values())

    for o in range(NZ):
        wait(("ra", o), pa.at[2, pl.ds(at_z(o - 1) * NY, NY)])
    for r in range(NY):
        wait(("rb", r), pb.at[2, pl.ds(at_y(r) * NZ, NZ)])
    for p in range(NT):
        pair = []
        for d in (2 * p, 2 * p + 1):
            i = (d % NY) * NZ + d // NY
            pair.append((pa[0, d] + pa[2, d]) + (pb[0, i] + pb[2, i]))
        sbuf[p] = jnp.concatenate(pair, axis=0)
    for r in range(1, NT):
        p = at_t(r)
        send(("p", r), sbuf.at[p], precv.at[me], (dp, p))
    precv[me] = sbuf[me]
    for r in range(1, NT):
        wait(("p", r), precv.at[at_t(-r)])
    projected = precv[0]
    for t in range(1, NT):
        projected = projected + precv[t]

    inner = lax.dot_general(
        projected, rows, nt, precision=lax.Precision.HIGHEST, preferred_element_type=F32
    )
    square = jnp.broadcast_to(jnp.sum(projected * projected, axis=1, keepdims=True), (16, 128))
    for i in range(NY):
        up_rows, lanes = slice((i // 2) * 8, (i // 2) * 8 + 8), slice((i % 2) * 128, (i % 2) * 128 + 128)
        y1s[i, 0] = inner[up_rows, lanes]
        y1s[i, 1] = square[up_rows, :]
    for r in range(1, NY):
        send(("y1", r), y1s.at[at_y(r)], y1r.at[y], dev(z, at_y(r)))
    y1r[y] = y1s[y]
    for r in range(1, NY):
        wait(("y1", r), y1r.at[at_y(-r)])
    z1r[z] = (y1r[0] + y1r[1]) + (y1r[2] + y1r[3])
    for r in range(1, NZ):
        send(("z1", r), z1r.at[z], z1r.at[z], dev(at_z(r), y))
    for r in range(1, NZ):
        wait(("tz", r), tqz.at[at_z(-r)])
    norm = tqz[0]
    for t in range(1, NZ):
        norm = norm + tqz[t]
    norm = jnp.where(lax.rem(y, 2) == 0, norm[0:1], norm[1:2])
    for r in range(1, NZ):
        wait(("z1", r), z1r.at[at_z(-r)])
    both = z1r[0]
    for t in range(1, NZ):
        both = both + z1r[t]
    fin[y] = math.sqrt(K) * both[0] * lax.rsqrt(both[1] + EPS) * lax.rsqrt(norm + EPS)
    for r in range(1, NY):
        send(("y2", r), fin.at[y], fin.at[y], dev(z, at_y(r)))
    for r in range(1, NY):
        wait(("y2", r), fin.at[at_y(-r)])
    for i in range(NY):
        out[(i // 2) * 8 : (i // 2) * 8 + 8, (i % 2) * 128 : (i % 2) * 128 + 128] = fin[i]
    for c in sent:
        c.wait_send()


def body(activations, cotangents, lengths, down, up, projection, target):
    vmem, hbm = pl.BlockSpec(memory_space=pltpu.VMEM), pl.BlockSpec(memory_space=pl.ANY)
    return pl.pallas_call(
        kernel,
        out_shape=jax.ShapeDtypeStruct((16, 256), F32),
        in_specs=[hbm] * 7,
        out_specs=vmem,
        scratch_shapes=[
            pltpu.VMEM((8, 128, 512), BF16),
            pltpu.VMEM((8, 128, 512), BF16),
            pltpu.SMEM((8,), jnp.int32),
            pltpu.VMEM((8, 512), BF16),
            pltpu.VMEM((8, 512), BF16),
            pltpu.VMEM((8192, 128), BF16),
            pltpu.VMEM((256, 128), BF16),
            pltpu.VMEM((4, W, 256), BF16),
            pltpu.VMEM((2, 2048, 128), BF16),
            pltpu.VMEM((4, 16, W), BF16),
            pltpu.VMEM((3, 16, W), BF16),
            pltpu.VMEM((32, 16, W), BF16),
            pltpu.VMEM((32, 16, W), BF16),
            pltpu.VMEM((16, 8, 128), F32),
            pltpu.VMEM((16, 8, 128), F32),
            pltpu.VMEM((16, 8, 128), F32),
            pltpu.VMEM((3, 32, 8, 128), F32),
            pltpu.VMEM((3, 32, 8, 128), F32),
            pltpu.VMEM((16, 16, 128), F32),
            pltpu.VMEM((16, 16, 128), F32),
            pltpu.VMEM((8, 128), F32),
            pltpu.VMEM((4, 8, 128), F32),
            pltpu.VMEM((8, 8, 128), F32),
            pltpu.VMEM((4, 2, 8, 128), F32),
            pltpu.VMEM((4, 2, 8, 128), F32),
            pltpu.VMEM((8, 2, 8, 128), F32),
            pltpu.VMEM((4, 8, 128), F32),
            pltpu.SemaphoreType.DMA((7,)),
            pltpu.SemaphoreType.DMA((len(TAGS),)),
            pltpu.SemaphoreType.DMA((len(TAGS),)),
        ],
        compiler_params=pltpu.CompilerParams(
            collective_id=0, has_side_effects=True, vmem_limit_bytes=60 * 1024 * 1024
        ),
    )(activations, cotangents, lengths, down.T, up, projection, target)


def solution(mesh):
    placed = (
        P("dp", None, "tensor"),
        P("dp", None, "tensor"),
        P("dp"),
        P("tensor", None),
        P(None, "tensor"),
        P("tensor", "dp"),
        P(None, "dp"),
    )
    return jax.shard_map(
        body, mesh=mesh, in_specs=placed, out_specs=P("tensor", None), check_vma=False
    )
```

time: 92.3 us -> 80.8 us (0.88)
  local copies, waits for them, and re-layouts: 7.53 us -> 1.32 us
  Pallas kernels: 83.3 us -> 78.2 us
    unnamed x15 -> x1, local copies, waits for them, and re-layouts: 7.53 us -> 1.32 us
    pallas_call x1, Pallas kernels: 83.3 us -> 78.2 us  [body(): pl.pallas_call(kernel, out_shape=jax.ShapeDtypeStruct((16, 256), F32), in...]
where the time goes in v2:
time: 80.8 us; the launch traced here: 79.5 us
  Pallas kernels  78.2 us (97%)
  local copies, waits for them, and re-layouts  1.32 us (2%)
    pallas_call x1, Pallas kernels, body(): pl.pallas_call(kernel, out_shape=jax.ShapeDtypeStruct((16, 256), F32), in...  78.2 us

profile of v2, /device:TPU:6, one launch (start us, length us, event | category | flops | bytes accessed | tf_op | source)
XLA Modules:
  0.0 79.5 jit_solution(2478773646271695325)
XLA Ops:
  0.0 78.2 %shard_map.73 = f32[16,256]{1,0:T(8,128)} custom-call(bf16[8,128,512]{2,1,0:T(8,128)(2,1)} %act_in.1, bf16[8,128,512]{2,1,0:T(8,128)(2,1)} %cot_in.1, s32[8]{0:T(128)} %lengths_in.1, bf16[8,512]{1,0:T(8,128)(2,1)} %bitcast.1, bf16[8,512]{1,0:T(8,128)(2,1)} %up_in.1, bf16[8192,128]{1,0:T(8,128)(2,1)} %proj_in.1, bf16[256,128]{1,0:T(8,128)(2,1)} %target_in.1), custom_call_target="tpu_custom_call" | custom-call | tf_op jit(solution)/shard_map/pallas_call | solution.py:367
  78.2 1.3 %copy.9 = f32[16,256]{1,0:T(8,128)} copy(f32[16,256]{1,0:T(8,128)} %shard_map.73) | data formatting | bytes 32768

commit v3 on v2

--- a/solution.py
+++ b/solution.py
@@ -66,19 +66,36 @@
 
 
 ORDER = [(tag, sends) for _, tag, sends in plan()]
+CUTS = (10, 10, 8, 4)
+
+
+def filled(tag):
+    kind = tag[0]
+    if kind == "own":
+        return [(0, 0, 0), (1, 0, 0)]
+    if kind == "Ay":
+        return [(0, 0, tag[2])] if tag[1] == "s" else []
+    if kind == "Az":
+        return [(0, tag[2], tag[1])]
+    if kind == "Bz":
+        return [(1, tag[1], 0)]
+    return [(1, tag[2], 2 if kind == "Bo" else 3 if tag[1] == "+" else 1)]
+
+
+COME = [[b[1:] for tag, _ in ORDER for b in filled(tag) if b[0] == half] for half in (0, 1)]
+STARTS = [sum(CUTS[:i]) for i in range(len(CUTS))]
 TAGS = [tag for tag, _ in ORDER[1:]]
-TAGS += [(k, r) for k in ("h", "f", "p") for r in range(1, NT)]
-TAGS += [(k, r) for k in ("y1", "y2", "ty") for r in range(1, NY)]
+TAGS += [(k, r) for k in ("h", "f") for r in range(1, NT)]
+TAGS += [(k, r) for k in ("y1", "ty") for r in range(1, NY)]
 TAGS += [(k, r) for k in ("z1", "tz") for r in range(1, NZ)]
-TAGS += [("pu",), ("pd",)] + [("ra", o) for o in range(NZ)] + [("rb", r) for r in range(NY)]
+TAGS += [("pu",), ("pd",)] + [("p", i, r) for i in range(3) for r in range(NT) if i or r]
 INDEX = {tag: i for i, tag in enumerate(TAGS)}
 
 
 def kernel(
     act_in, cot_in, lengths_in, down_in, up_in, proj_in, target_in, out,
-    act, cot, lengths, down, up, proj, target, pc, neighbours, own_blocks, other, ga, gb, hid, hrecv, facs, pa, pb,
-    sbuf, precv,
-    tq, tqy, tqz, y1s, y1r, z1r, fin, lsem, ssem, rsem,
+    act, cot, lengths, down, up, proj, target, pc, neighbours, own_blocks, other, ga, gb, hid, hrecv, facs, total, rounded, precv,
+    tqz, along, zsum, lsem, ssem, rsem,
 ):
     dp, me = lax.axis_index("dp"), lax.axis_index("tensor")
     z, y = lax.div(dp, NY), lax.rem(dp, NY)
@@ -113,9 +130,10 @@
     def wait(tag, ref):
         copy(tag, ref, ref, dev(at_z(1), y)).wait_recv()
 
+    here_y = pl.ds(pl.multiple_of(y * 128, 128), 128)
     ends = (
         (down_in, down), (act_in, act), (up_in, up), (cot_in, cot),
-        (target_in, target), (lengths_in, lengths), (proj_in, proj),
+        (target_in, target.at[:, here_y]), (lengths_in, lengths), (proj_in, proj),
     )
     loads = [pltpu.make_async_copy(a, b, lsem.at[i]) for i, (a, b) in enumerate(ends)]
     for c in loads:
@@ -124,6 +142,7 @@
     barrier = pltpu.get_barrier_semaphore()
     partners = [(dp, at_t(r)) for r in range(1, NT)]
     partners += [dev(at_z(o), y) for o in range(1, NZ)] + [dev(z, at_y(o)) for o in range(1, NY)]
+    partners += [(at_z(o) * NY + y, at_t(r)) for o in (-1, 1) for r in range(1, NT)]
     for p in partners:
         pl.semaphore_signal(barrier, inc=1, device_id=p, device_id_type=MESH)
 
@@ -147,16 +166,8 @@
     hrecv[me] = hid[me]
 
     loads[4].wait()
-    rows = target[...].astype(F32)
-    ones = jnp.ones((8, 128), F32)
-    norms = lax.dot_general(
-        ones, rows * rows, nt, precision=lax.Precision.HIGHEST, preferred_element_type=F32
-    )
-    which = lax.broadcasted_iota(jnp.int32, (8, 128), 0)
-    tq[...] = jnp.where(which == 0, norms[:, :128], norms[:, 128:])
     for r in range(1, NY):
-        send(("ty", r), tq, tqy.at[y], dev(z, at_y(r)))
-    tqy[y] = tq[...]
+        send(("ty", r), target.at[:, here_y], target.at[:, here_y], dev(z, at_y(r)))
 
     q = lax.broadcasted_iota(jnp.int32, (256, 256), 0)
     c = lax.broadcasted_iota(jnp.int32, (256, 256), 1)
@@ -175,24 +186,20 @@
 
     mine = pl.multiple_of(parity * 4096, 4096)
     turn(proj, mine, pc.at[0])
-    turn(proj, mine + 2048, pc.at[1])
 
     for r in range(1, NT):
         wait(("h", r), hrecv.at[at_t(-r)])
-    total = hrecv[0]
+    hidden = hrecv[0]
     for t in range(1, NT):
-        total = total + hrecv[t]
+        hidden = hidden + hrecv[t]
     loads[5].wait()
     token = lax.broadcasted_iota(jnp.int32, (8, 128), 1)
-    facs[me] = jnp.where(token < lengths[lax.rem(me, 8)], SCALE, 0.0) * total
+    facs[me] = jnp.where(token < lengths[lax.rem(me, 8)], SCALE, 0.0) * hidden
     for r in range(1, NT):
         send(("f", r), facs.at[me], facs.at[me], (dp, at_t(r)))
 
-    for r in range(1, NY):
-        wait(("ty", r), tqy.at[at_y(-r)])
-    tqz[z] = (tqy[0] + tqy[1]) + (tqy[2] + tqy[3])
-    for r in range(1, NZ):
-        send(("tz", r), tqz.at[z], tqz.at[z], dev(at_z(r), y))
+    turn(proj, mine + 2048, pc.at[1])
+    total[...] = jnp.zeros((3, 32, 8, 128), F32)
 
     for r in range(1, NT):
         wait(("f", r), facs.at[at_t(-r)])
@@ -213,11 +220,17 @@
     ga[dp] = own_blocks[same]
     gb[y * NZ + z] = own_blocks[same + 1]
 
+    def slot_index_a(o, r):
+        return at_z(o) * NY + at_y(r)
+
+    def slot_index_b(o, r):
+        return at_y(r) * NZ + at_z(o)
+
     def slot_a(o, r):
-        return ga.at[at_z(o) * NY + at_y(r)]
+        return ga.at[slot_index_a(o, r)]
 
     def slot_b(o, r):
-        return gb.at[at_y(r) * NZ + at_z(o)]
+        return gb.at[slot_index_b(o, r)]
 
     def slot(tag):
         kind = tag[0]
@@ -256,34 +269,31 @@
         found = found.reshape(-1, 2, 8, 256)
         return found[:, 0, :, :128] + found[:, 1, :, 128:]
 
-    def product_a(o):
-        at = pl.ds(at_z(o) * NY, NY)
-        block = ga[at].reshape(NY * 16, W)
-        pa[1, at] = fold(jnp.dot(block, pc[2], preferred_element_type=F32))
-        send(("ra", o), pa.at[1, at], pa.at[2, at], dev(at_z(1), y))
-        pa[0, at] = fold(jnp.dot(block, pc[0], preferred_element_type=F32))
-
-    def product_b(r):
-        at = pl.ds(at_y(r) * NZ, NZ)
-        block = gb[at].reshape(NZ * 16, W)
-        pb[1, at] = fold(jnp.dot(block, pc[3], preferred_element_type=F32))
-        send(("rb", r), pb.at[1, at], pb.at[2, at], dev(at_z(-1), y))
-        pb[0, at] = fold(jnp.dot(block, pc[1], preferred_element_type=F32))
-
-    come = []
-
-    def products(run, which):
-        if not come:
-            wait(("pu",), neighbours.at[0])
-            turn(neighbours.at[0], 0, pc.at[2])
-            wait(("pd",), neighbours.at[1])
-            turn(neighbours.at[1], 0, pc.at[3])
-        come.append(run)
-        run(which)
-
-    need_a = {o: 4 for o in range(NZ)}
-    need_b = {r: 8 for r in range(NY)}
-    for tag, sends in ORDER:
+    def product(half, first, count):
+        gathered, slots = ((ga, slot_index_a), (gb, slot_index_b))[half]
+        places = COME[half][first : first + count]
+        block = jnp.concatenate([gathered[slots(o, r)] for o, r in places], axis=0)
+        mine = fold(jnp.dot(block, pc[half], preferred_element_type=F32))
+        next_one = fold(jnp.dot(block, pc[2 + half], preferred_element_type=F32))
+        for i, (o, r) in enumerate(places):
+            at = slot_index_a(o, r)
+            total[0, at] += mine[i]
+            total[1 + half, at] = next_one[i]
+
+    def validation():
+        for r in range(1, NY):
+            lanes = pl.ds(pl.multiple_of(at_y(-r) * 128, 128), 128)
+            wait(("ty", r), target.at[:, lanes])
+        ones = jnp.ones((8, 512), F32)
+        wide = target[...].astype(F32)
+        tqz[z] = lax.dot_general(
+            ones, wide * wide, nt, precision=lax.Precision.HIGHEST, preferred_element_type=F32
+        )
+        for r in range(1, NZ):
+            send(("tz", r), tqz.at[z], tqz.at[z], dev(at_z(r), y))
+
+    seen = [0, 0]
+    for turn_of, (tag, sends) in enumerate(ORDER):
         if tag != ("own",):
             wait(tag, slot(tag))
         for link, new in sends:
@@ -291,73 +301,64 @@
             step = links if link[1] == "+" else -links
             to = dev(at_z(step), y) if link[0] == "z" else dev(z, at_y(step))
             send(new, *ends_of(link, new), to)
-        kind = tag[0]
-        if kind in ("own", "Ay", "Az") and tag[1:2] != ("o",):
-            o = tag[2] % NZ if kind == "Az" else 0
-            need_a[o] -= 1
-            if need_a[o] == 0:
-                products(product_a, o)
-        if kind in ("own", "Bz", "By", "Bo"):
-            r = 2 if kind == "Bo" else 0 if kind != "By" else 3 if tag[1] == "+" else 1
-            need_b[r] -= 1
-            if need_b[r] == 0:
-                products(product_b, r)
-    assert not any(need_a.values()) and not any(need_b.values())
-
-    for o in range(NZ):
-        wait(("ra", o), pa.at[2, pl.ds(at_z(o - 1) * NY, NY)])
-    for r in range(NY):
-        wait(("rb", r), pb.at[2, pl.ds(at_y(r) * NZ, NZ)])
-    for p in range(NT):
-        pair = []
-        for d in (2 * p, 2 * p + 1):
-            i = (d % NY) * NZ + d // NY
-            pair.append((pa[0, d] + pa[2, d]) + (pb[0, i] + pb[2, i]))
-        sbuf[p] = jnp.concatenate(pair, axis=0)
-    for r in range(1, NT):
-        p = at_t(r)
-        send(("p", r), sbuf.at[p], precv.at[me], (dp, p))
-    precv[me] = sbuf[me]
-    for r in range(1, NT):
-        wait(("p", r), precv.at[at_t(-r)])
-    projected = precv[0]
-    for t in range(1, NT):
-        projected = projected + precv[t]
-
-    inner = lax.dot_general(
-        projected, rows, nt, precision=lax.Precision.HIGHEST, preferred_element_type=F32
+        if turn_of == 8:
+            validation()
+        for half, _, _ in filled(tag):
+            seen[half] += 1
+            for first, count in zip(STARTS, CUTS):
+                if seen[half] == first + count:
+                    if first == 0:
+                        wait(("pd",) if half else ("pu",), neighbours.at[half])
+                        turn(neighbours.at[half], 0, pc.at[2 + half])
+                    product(half, first, count)
+
+    for i, o in ((1, 1), (2, -1), (0, 0)):
+        rounded[i] = total[i].reshape(16, 16, 128).astype(BF16)
+        for r in range(NT):
+            if i or r:
+                p = at_t(r)
+                send(("p", i, r), rounded.at[i, p], precv.at[i, me], (at_z(o) * NY + y, p))
+    precv[0, me] = rounded[0, me]
+    projected = jnp.zeros((16, 128), F32)
+    for i in (1, 2, 0):
+        for r in range(NT):
+            if i or r:
+                wait(("p", i, r), precv.at[i, at_t(-r)])
+    for i in range(3):
+        for t in range(NT):
+            projected = projected + precv[i, t].astype(F32)
+    along[y] = projected
+    for r in range(1, NY):
+        send(("y1", r), along.at[y], along.at[y], dev(z, at_y(r)))
+    for r in range(1, NY):
+        wait(("y1", r), along.at[at_y(-r)])
+    wide = jnp.concatenate([along[i] for i in range(NY)], axis=1)
+    high = wide.astype(BF16)
+    rest = wide - high.astype(F32)
+    middle = rest.astype(BF16)
+    low = (rest - middle.astype(F32)).astype(BF16)
+    three = lax.dot_general(
+        jnp.concatenate([high, middle, low], axis=0), target[...], nt, preferred_element_type=F32
     )
-    square = jnp.broadcast_to(jnp.sum(projected * projected, axis=1, keepdims=True), (16, 128))
-    for i in range(NY):
-        up_rows, lanes = slice((i // 2) * 8, (i // 2) * 8 + 8), slice((i % 2) * 128, (i % 2) * 128 + 128)
-        y1s[i, 0] = inner[up_rows, lanes]
-        y1s[i, 1] = square[up_rows, :]
-    for r in range(1, NY):
-        send(("y1", r), y1s.at[at_y(r)], y1r.at[y], dev(z, at_y(r)))
-    y1r[y] = y1s[y]
-    for r in range(1, NY):
-        wait(("y1", r), y1r.at[at_y(-r)])
-    z1r[z] = (y1r[0] + y1r[1]) + (y1r[2] + y1r[3])
+    zsum[z, :, :256] = ((three[32:] + three[16:32]) + three[:16]).astype(BF16)
+    square = jnp.sum(wide * wide, axis=1, keepdims=True)
+    zsum[z, :, 256:] = jnp.broadcast_to(square, (16, 128)).astype(BF16)
     for r in range(1, NZ):
-        send(("z1", r), z1r.at[z], z1r.at[z], dev(at_z(r), y))
+        send(("z1", r), zsum.at[z], zsum.at[z], dev(at_z(r), y))
     for r in range(1, NZ):
         wait(("tz", r), tqz.at[at_z(-r)])
     norm = tqz[0]
     for t in range(1, NZ):
         norm = norm + tqz[t]
-    norm = jnp.where(lax.rem(y, 2) == 0, norm[0:1], norm[1:2])
+    norm = math.sqrt(K) * lax.rsqrt(norm[0:1] + EPS)
     for r in range(1, NZ):
-        wait(("z1", r), z1r.at[at_z(-r)])
-    both = z1r[0]
+        wait(("z1", r), zsum.at[at_z(-r)])
+    both = zsum[0].astype(F32)
     for t in range(1, NZ):
-        both = both + z1r[t]
-    fin[y] = math.sqrt(K) * both[0] * lax.rsqrt(both[1] + EPS) * lax.rsqrt(norm + EPS)
-    for r in range(1, NY):
-        send(("y2", r), fin.at[y], fin.at[y], dev(z, at_y(r)))
-    for r in range(1, NY):
-        wait(("y2", r), fin.at[at_y(-r)])
-    for i in range(NY):
-        out[(i // 2) * 8 : (i // 2) * 8 + 8, (i % 2) * 128 : (i % 2) * 128 + 128] = fin[i]
+        both = both + zsum[t].astype(F32)
+    own_norm = lax.rsqrt(both[:, 256:] + EPS)
+    out[:, :128] = both[:, :128] * own_norm * norm[:, :128]
+    out[:, 128:] = both[:, 128:256] * own_norm * norm[:, 128:]
     for c in sent:
         c.wait_send()
 
@@ -376,7 +377,7 @@
             pltpu.VMEM((8, 512), BF16),
             pltpu.VMEM((8, 512), BF16),
             pltpu.VMEM((8192, 128), BF16),
-            pltpu.VMEM((256, 128), BF16),
+            pltpu.VMEM((256, 512), BF16),
             pltpu.VMEM((4, W, 256), BF16),
             pltpu.VMEM((2, 2048, 128), BF16),
             pltpu.VMEM((4, 16, W), BF16),
@@ -387,16 +388,11 @@
             pltpu.VMEM((16, 8, 128), F32),
             pltpu.VMEM((16, 8, 128), F32),
             pltpu.VMEM((3, 32, 8, 128), F32),
-            pltpu.VMEM((3, 32, 8, 128), F32),
-            pltpu.VMEM((16, 16, 128), F32),
-            pltpu.VMEM((16, 16, 128), F32),
-            pltpu.VMEM((8, 128), F32),
-            pltpu.VMEM((4, 8, 128), F32),
-            pltpu.VMEM((8, 8, 128), F32),
-            pltpu.VMEM((4, 2, 8, 128), F32),
-            pltpu.VMEM((4, 2, 8, 128), F32),
-            pltpu.VMEM((8, 2, 8, 128), F32),
-            pltpu.VMEM((4, 8, 128), F32),
+            pltpu.VMEM((3, 16, 16, 128), BF16),
+            pltpu.VMEM((3, 16, 16, 128), BF16),
+            pltpu.VMEM((8, 8, 256), F32),
+            pltpu.VMEM((4, 16, 128), F32),
+            pltpu.VMEM((8, 16, 384), BF16),
             pltpu.SemaphoreType.DMA((7,)),
             pltpu.SemaphoreType.DMA((len(TAGS),)),
             pltpu.SemaphoreType.DMA((len(TAGS),)),

time: 80.8 us -> 74.6 us (0.923); the launches traced: 79.5 us -> 74.4 us
  Pallas kernels: 78.2 us -> 73 us
    pallas_call x1, Pallas kernels: 78.2 us -> 73 us  [body(): pl.pallas_call(kernel, out_shape=jax.ShapeDtypeStruct((16, 256), F32), in...]
where the time goes in v3:
time: 74.6 us; the launch traced here: 74.4 us
  Pallas kernels  73 us (98%)
  local copies, waits for them, and re-layouts  1.32 us (2%)
    pallas_call x1, Pallas kernels, body(): pl.pallas_call(kernel, out_shape=jax.ShapeDtypeStruct((16, 256), F32), in...  73 us

profile of v3, /device:TPU:6, one launch (start us, length us, event | category | flops | bytes accessed | tf_op | source)
XLA Modules:
  0.0 74.4 jit_solution(9608664929632450284)
XLA Ops:
  0.0 73.0 %shard_map.73 = f32[16,256]{1,0:T(8,128)} custom-call(bf16[8,128,512]{2,1,0:T(8,128)(2,1)} %act_in.1, bf16[8,128,512]{2,1,0:T(8,128)(2,1)} %cot_in.1, s32[8]{0:T(128)} %lengths_in.1, bf16[8,512]{1,0:T(8,128)(2,1)} %bitcast.1, bf16[8,512]{1,0:T(8,128)(2,1)} %up_in.1, bf16[8192,128]{1,0:T(8,128)(2,1)} %proj_in.1, bf16[256,128]{1,0:T(8,128)(2,1)} %target_in.1), custom_call_target="tpu_custom_call" | custom-call | tf_op jit(solution)/shard_map/pallas_call | solution.py:368
  73.0 1.3 %copy.9 = f32[16,256]{1,0:T(8,128)} copy(f32[16,256]{1,0:T(8,128)} %shard_map.73) | data formatting | bytes 32768

commit v4 on v3

--- a/solution.py
+++ b/solution.py
@@ -51,21 +51,42 @@
     return []
 
 
+def left(tag):
+    return max((n * 1.255 + 2.2 + left(new) for _, new, n in follow(tag)), default=0.0)
+
+
+BUSY, AHEAD = 2.0, 2.5
+
+
 def plan():
-    free = dict.fromkeys(("z+", "z-", "y+", "y-"), 0.0)
-    heap, order, count = [(0.0, 0, ("own",))], [], 0
+    free = {"z+": BUSY, "z-": BUSY, "y+": 0.0, "y-": 0.0}
+    waiting = {link: [] for link in free}
+    heap, count, came, starts = [(0.0, 0, ("own",)), (BUSY, 1, None)], 1, {}, []
     while heap:
-        now, _, tag = heapq.heappop(heap)
-        sends = follow(tag)
-        order.append((now, tag, [(link, new) for link, new, _ in sends]))
-        for link, new, links in sends:
-            count += 1
-            free[link] = max(now, free[link]) + links * 0.655
-            heapq.heappush(heap, (free[link] + 2.2 + 0.6 * links, count, new))
+        now = heap[0][0]
+        while heap and heap[0][0] <= now + 1e-6:
+            tag = heapq.heappop(heap)[2]
+            if tag is not None:
+                came[tag] = now
+                for link, new, links in follow(tag):
+                    count += 1
+                    heapq.heappush(waiting[link], (-left(new), count, new, links, now))
+        for link, line in waiting.items():
+            if line and free[link] <= now + 1e-6:
+                _, _, new, links, since = heapq.heappop(line)
+                free[link] = now + links * 0.655
+                starts.append((max(since, now - AHEAD), now, link, new))
+                count += 2
+                heapq.heappush(heap, (free[link], count - 1, None))
+                heapq.heappush(heap, (free[link] + 2.2 + 0.6 * links, count, new))
+    order = [(tag, []) for tag in came]
+    times = list(came.values())
+    for issue, _, link, new in sorted(starts, key=lambda x: x[1]):
+        order[sum(t <= issue + 1e-6 for t in times) - 1][1].append((link, new))
     return order
 
 
-ORDER = [(tag, sends) for _, tag, sends in plan()]
+ORDER = plan()
 CUTS = (10, 10, 8, 4)
 
 
@@ -88,13 +109,13 @@
 TAGS += [(k, r) for k in ("h", "f") for r in range(1, NT)]
 TAGS += [(k, r) for k in ("y1", "ty") for r in range(1, NY)]
 TAGS += [(k, r) for k in ("z1", "tz") for r in range(1, NZ)]
-TAGS += [("pu",), ("pd",)] + [("p", i, r) for i in range(3) for r in range(NT) if i or r]
+TAGS += [("pu",), ("pd",)] + [("c",)] + [("p", i, r) for i in range(3) for r in range(8) if i or r]
 INDEX = {tag: i for i, tag in enumerate(TAGS)}
 
 
 def kernel(
     act_in, cot_in, lengths_in, down_in, up_in, proj_in, target_in, out,
-    act, cot, lengths, down, up, proj, target, pc, neighbours, own_blocks, other, ga, gb, hid, hrecv, facs, total, rounded, precv,
+    act, cot, lengths, down, up, proj, target, pc, neighbours, own_blocks, other, ga, gb, hid, hrecv, facs, total, twin, rounded, precv,
     tqz, along, zsum, lsem, ssem, rsem,
 ):
     dp, me = lax.axis_index("dp"), lax.axis_index("tensor")
@@ -126,6 +147,11 @@
         c = copy(tag, src, dst, device)
         c.start()
         sent.append(c)
+
+    def settle(some):
+        for c in sent[:some]:
+            c.wait_send()
+        del sent[:some]
 
     def wait(tag, ref):
         copy(tag, ref, ref, dev(at_z(1), y)).wait_recv()
@@ -142,7 +168,7 @@
     barrier = pltpu.get_barrier_semaphore()
     partners = [(dp, at_t(r)) for r in range(1, NT)]
     partners += [dev(at_z(o), y) for o in range(1, NZ)] + [dev(z, at_y(o)) for o in range(1, NY)]
-    partners += [(at_z(o) * NY + y, at_t(r)) for o in (-1, 1) for r in range(1, NT)]
+    partners += [(at_z(o) * NY + y, at_t(r)) for o in (-1, 1) for r in range(2, NT, 2)]
     for p in partners:
         pl.semaphore_signal(barrier, inc=1, device_id=p, device_id_type=MESH)
 
@@ -198,8 +224,9 @@
     for r in range(1, NT):
         send(("f", r), facs.at[me], facs.at[me], (dp, at_t(r)))
 
+    settle(NT - 1)
     turn(proj, mine + 2048, pc.at[1])
-    total[...] = jnp.zeros((3, 32, 8, 128), F32)
+    total[...] = jnp.zeros((2, 3, 8, 2, 8, 128), F32)
 
     for r in range(1, NT):
         wait(("f", r), facs.at[at_t(-r)])
@@ -276,9 +303,9 @@
         mine = fold(jnp.dot(block, pc[half], preferred_element_type=F32))
         next_one = fold(jnp.dot(block, pc[2 + half], preferred_element_type=F32))
         for i, (o, r) in enumerate(places):
-            at = slot_index_a(o, r)
-            total[0, at] += mine[i]
-            total[1 + half, at] = next_one[i]
+            core_of, pair = lax.div(at_y(r), 2), lax.rem(at_y(r), 2)
+            total[core_of, 0, at_z(o), pair] += mine[i]
+            total[core_of, 1 + half, at_z(o), pair] = next_one[i]
 
     def validation():
         for r in range(1, NY):
@@ -312,20 +339,26 @@
                         turn(neighbours.at[half], 0, pc.at[2 + half])
                     product(half, first, count)
 
+    core, spot = lax.rem(me, 2), lax.div(me, 2)
+    send(("c",), total.at[1 - core], twin, (dp, me + 1 - 2 * core))
+    wait(("c",), twin)
     for i, o in ((1, 1), (2, -1), (0, 0)):
-        rounded[i] = total[i].reshape(16, 16, 128).astype(BF16)
-        for r in range(NT):
+        both_cores = total[core, i] + twin[i]
+        rounded[i] = both_cores.reshape(8, 16, 128).astype(BF16)
+        for r in range(8):
             if i or r:
-                p = at_t(r)
-                send(("p", i, r), rounded.at[i, p], precv.at[i, me], (at_z(o) * NY + y, p))
-    precv[0, me] = rounded[0, me]
+                q = lax.rem(spot + r, 8)
+                to = (at_z(o) * NY + y, q * 2 + core)
+                send(("p", i, r), rounded.at[i, q], precv.at[i, spot], to)
+    settle(len(sent))
+    precv[0, spot] = rounded[0, spot]
     projected = jnp.zeros((16, 128), F32)
     for i in (1, 2, 0):
-        for r in range(NT):
+        for r in range(8):
             if i or r:
-                wait(("p", i, r), precv.at[i, at_t(-r)])
+                wait(("p", i, r), precv.at[i, lax.rem(spot + 8 - r, 8)])
     for i in range(3):
-        for t in range(NT):
+        for t in range(8):
             projected = projected + precv[i, t].astype(F32)
     along[y] = projected
     for r in range(1, NY):
@@ -345,6 +378,7 @@
     zsum[z, :, 256:] = jnp.broadcast_to(square, (16, 128)).astype(BF16)
     for r in range(1, NZ):
         send(("z1", r), zsum.at[z], zsum.at[z], dev(at_z(r), y))
+    settle(len(sent) - NZ + 1)
     for r in range(1, NZ):
         wait(("tz", r), tqz.at[at_z(-r)])
     norm = tqz[0]
@@ -359,8 +393,7 @@
     own_norm = lax.rsqrt(both[:, 256:] + EPS)
     out[:, :128] = both[:, :128] * own_norm * norm[:, :128]
     out[:, 128:] = both[:, 128:256] * own_norm * norm[:, 128:]
-    for c in sent:
-        c.wait_send()
+    settle(len(sent))
 
 
 def body(activations, cotangents, lengths, down, up, projection, target):
@@ -387,9 +420,10 @@
             pltpu.VMEM((16, 8, 128), F32),
             pltpu.VMEM((16, 8, 128), F32),
             pltpu.VMEM((16, 8, 128), F32),
-            pltpu.VMEM((3, 32, 8, 128), F32),
-            pltpu.VMEM((3, 16, 16, 128), BF16),
-            pltpu.VMEM((3, 16, 16, 128), BF16),
+            pltpu.VMEM((2, 3, 8, 2, 8, 128), F32),
+            pltpu.VMEM((3, 8, 2, 8, 128), F32),
+            pltpu.VMEM((3, 8, 16, 128), BF16),
+            pltpu.VMEM((3, 8, 16, 128), BF16),
             pltpu.VMEM((8, 8, 256), F32),
             pltpu.VMEM((4, 16, 128), F32),
             pltpu.VMEM((8, 16, 384), BF16),

time: 74.6 us -> 71.5 us (0.958)
  Pallas kernels: 73 us -> 69.9 us
    pallas_call x1, Pallas kernels: 73 us -> 69.9 us  [body(): pl.pallas_call(kernel, out_shape=jax.ShapeDtypeStruct((16, 256), F32), in...]
where the time goes in v4:
time: 71.5 us; the launch traced here: 71.3 us
  Pallas kernels  69.9 us (98%)
  local copies, waits for them, and re-layouts  1.32 us (2%)
    pallas_call x1, Pallas kernels, body(): pl.pallas_call(kernel, out_shape=jax.ShapeDtypeStruct((16, 256), F32), in...  69.9 us

profile of v4, /device:TPU:6, one launch (start us, length us, event | category | flops | bytes accessed | tf_op | source)
XLA Modules:
  0.0 71.3 jit_solution(17512719875674302637)
XLA Ops:
  0.0 69.9 %shard_map.73 = f32[16,256]{1,0:T(8,128)} custom-call(bf16[8,128,512]{2,1,0:T(8,128)(2,1)} %act_in.1, bf16[8,128,512]{2,1,0:T(8,128)(2,1)} %cot_in.1, s32[8]{0:T(128)} %lengths_in.1, bf16[8,512]{1,0:T(8,128)(2,1)} %bitcast.1, bf16[8,512]{1,0:T(8,128)(2,1)} %up_in.1, bf16[8192,128]{1,0:T(8,128)(2,1)} %proj_in.1, bf16[256,128]{1,0:T(8,128)(2,1)} %target_in.1), custom_call_target="tpu_custom_call" | custom-call | tf_op jit(solution)/shard_map/pallas_call | solution.py:401
  69.9 1.3 %copy.9 = f32[16,256]{1,0:T(8,128)} copy(f32[16,256]{1,0:T(8,128)} %shard_map.73) | data formatting | bytes 32768

commit v5 on v4

--- a/solution.py
+++ b/solution.py
@@ -320,7 +320,7 @@
             send(("tz", r), tqz.at[z], tqz.at[z], dev(at_z(r), y))
 
     seen = [0, 0]
-    for turn_of, (tag, sends) in enumerate(ORDER):
+    for tag, sends in ORDER:
         if tag != ("own",):
             wait(tag, slot(tag))
         for link, new in sends:
@@ -328,8 +328,6 @@
             step = links if link[1] == "+" else -links
             to = dev(at_z(step), y) if link[0] == "z" else dev(z, at_y(step))
             send(new, *ends_of(link, new), to)
-        if turn_of == 8:
-            validation()
         for half, _, _ in filled(tag):
             seen[half] += 1
             for first, count in zip(STARTS, CUTS):
@@ -350,7 +348,8 @@
                 q = lax.rem(spot + r, 8)
                 to = (at_z(o) * NY + y, q * 2 + core)
                 send(("p", i, r), rounded.at[i, q], precv.at[i, spot], to)
-    settle(len(sent))
+    validation()
+    settle(len(sent) - NZ + 1)
     precv[0, spot] = rounded[0, spot]
     projected = jnp.zeros((16, 128), F32)
     for i in (1, 2, 0):

time: 71.5 us -> 71.3 us (level); the launches traced: 71.3 us -> 70.3 us
  Pallas kernels: 69.9 us -> 69 us
    pallas_call x1, Pallas kernels: 69.9 us -> 69 us  [body(): pl.pallas_call(kernel, out_shape=jax.ShapeDtypeStruct((16, 256), F32), in...]
where the time goes in v5:
time: 71.3 us; the launch traced here: 70.3 us
  Pallas kernels  69 us (97%)
  local copies, waits for them, and re-layouts  1.32 us (2%)
    pallas_call x1, Pallas kernels, body(): pl.pallas_call(kernel, out_shape=jax.ShapeDtypeStruct((16, 256), F32), in...  69 us

profile of v5, /device:TPU:6, one launch (start us, length us, event | category | flops | bytes accessed | tf_op | source)
XLA Modules:
  0.0 70.3 jit_solution(9594927481312730113)
XLA Ops:
  0.0 69.0 %shard_map.73 = f32[16,256]{1,0:T(8,128)} custom-call(bf16[8,128,512]{2,1,0:T(8,128)(2,1)} %act_in.1, bf16[8,128,512]{2,1,0:T(8,128)(2,1)} %cot_in.1, s32[8]{0:T(128)} %lengths_in.1, bf16[8,512]{1,0:T(8,128)(2,1)} %bitcast.1, bf16[8,512]{1,0:T(8,128)(2,1)} %up_in.1, bf16[8192,128]{1,0:T(8,128)(2,1)} %proj_in.1, bf16[256,128]{1,0:T(8,128)(2,1)} %target_in.1), custom_call_target="tpu_custom_call" | custom-call | tf_op jit(solution)/shard_map/pallas_call | solution.py:400
  69.0 1.3 %copy.9 = f32[16,256]{1,0:T(8,128)} copy(f32[16,256]{1,0:T(8,128)} %shard_map.73) | data formatting | bytes 32768
